TPU v7x, 256 devices: a whole 4x4x8 slice. The times are simulated.
256 devices in a mesh: out: 8 (over x, y_hi), ap: 32 (over z, y_lo, core).
Axes of the slice: x: 4, y: 4 (y_hi: 2, y_lo: 2; y = y_hi * 2 + y_lo), z: 8, core: 2. Of those that a mesh axis runs over, the one named last changes fastest.
Arguments:
- panels: bfloat16 [1280, 256, 2, 1152], P('ap', 'out'), may hold values from -6 to 6
- shot_data: bfloat16 [16, 1280, 2, 1152], P('out', 'ap'), may hold values from -6 to 6
- taper_table: float32 [8, 32], replicated, may hold values from 0.2 to 1
- destination: int32 [8, 1280], P('out', 'ap'), may hold values from -1 to 31, as said below
- taper_level: int32 [8, 1280], P('out', 'ap'), may hold values from 0 to 7
- shot_order: int32 [4], replicated, may hold values from 0 to 15
Outputs:
- multiples: float32 [4, 256, 2, 1152], P(None, 'out', None, 'ap')
Inputs may be any that keep to these rules, and one draw needn't show every extreme that they name: For each batch, every index of ap is the destination of exactly 14 locations; the 40 locations stored at one index of ap send at most 2 to any one destination, and at some index all 40 are inside the aperture.
All inputs are finite; a program needn't handle non-finite values.
Results may differ from a plain program's by a relative error of at most 0.0003.
Values may be sent and summed in bfloat16 or wider, within the bound.
A program may use at most 128 MiB of HBM per device.

v0:
```python
import jax
import jax.numpy as jnp
from jax import lax
from jax.sharding import PartitionSpec as P

SHOTS = 4


def from_root(value, axis, source):
    kept = jnp.where(lax.axis_index(axis) == source, value, 0).astype(value.dtype)
    return lax.psum(kept, axis)


def taper_weights(taper_table, levels):
    count = taper_table.shape[0]
    onehot = (levels[:, None] == jnp.arange(count, dtype=jnp.int32)[None, :]).astype(jnp.float32)
    return jnp.dot(onehot, taper_table, precision=lax.Precision.HIGHEST)


def predicted(weights, traces, block):
    real_trace = traces[:, 0, :].astype(jnp.float32)[:, None, :]
    imag_trace = traces[:, 1, :].astype(jnp.float32)[:, None, :]
    real_panel = block[:, :, 0, :].astype(jnp.float32)
    imag_panel = block[:, :, 1, :].astype(jnp.float32)
    scale = weights[:, :, None]
    real_part = jnp.sum(scale * (real_trace * real_panel - imag_trace * imag_panel), axis=0)
    imag_part = jnp.sum(scale * (real_trace * imag_panel + imag_trace * real_panel), axis=0)
    return jnp.stack([real_part, imag_part], axis=1)


def on_device(panels, shot_data, taper_table, destination, taper_level, shot_order):
    per_source = shot_data.shape[0]
    local_dest = destination[0]
    local_level = taper_level[0]
    holder_weights = taper_weights(taper_table, jnp.where(local_dest >= 0, local_level, -1))
    totals = []
    for step in range(SHOTS):
        shot = shot_order[step]
        mine = lax.dynamic_index_in_dim(shot_data, shot % per_source, 0, keepdims=False)
        traces_here = from_root(mine, "out", shot // per_source)
        term = predicted(holder_weights, traces_here, panels)
        totals.append(lax.psum_scatter(term, "ap", scatter_dimension=2, tiled=True))
    return jnp.stack(totals, axis=0)


def solution(mesh):
    placed = (
        P("ap", "out", None, None),
        P("out", "ap", None, None),
        P(),
        P("out", "ap"),
        P("out", "ap"),
        P(),
    )
    return jax.shard_map(
        on_device, mesh=mesh, in_specs=placed, out_specs=P(None, "out", None, "ap"), check_vma=False
    )
```

profile of v0, /device:TPU:1, one launch (start us, length us, event | category | flops | bytes accessed | tf_op | source)
XLA Modules:
  0.0 370.0 jit_solution(8028032665125867469)
XLA Ops:
  6.5 0.0 copy-start
  6.5 0.0 all-reduce.11.cloned.1.call-start
  6.5 1.5 fusion.32
  18.2 2.7 fusion.27
  20.9 0.0 all-reduce.11.cloned.1.call-update
  20.9 0.0 copy-start.2
  21.0 0.0 copy-start.3
  21.0 0.0 all-reduce.9.cloned.1.call-start
  21.0 15.1 %fusion.31 = (bf16[40,32,1,1152]{3,2,1,0:T(2,128)(2,1)}, bf16[40,32,1,1152]{3,2,1,0:T(2,128)(2,1)}) fusion(bf16[40,32,2,1152]{3,2,1,0:T(2,128)(2,1)} %param.6), kind=kLoop, calls=%fused_computation.80 | loop fusion | bytes 11796480 | tf_op jit(solution)/shard_map/slice | solution.py:23
  36.1 0.0 copy-done.2
  36.1 0.0 copy-done.3
  36.1 0.0 copy-done
  36.2 0.2 fusion.28
  36.4 75.9 %all-reduce.11.cloned.1.call-done = (bf16[40,2,1152]{2,1,0:T(2,128)(2,1)}, bf16[40,2,1152]{2,1,0:T(2,128)(2,1)}, bf16[40,2,1152]{2,1,0:T(2,128)(2,1)}, bf16[40,2,1152]{2,1,0:T(2,128)(2,1)}) async-done(((bf16[40,2,1152]{2,1,0:T(2,128)(2,1)}, bf16[40,2,1152]{2,1,0:T(2,128)(2,1)}, bf16[40,2,1152]{2,1,0:T(2,128)(2,1)}, bf16[40,2,1152]{2,1,0:T(2,128)(2,1)}), (bf16[40,2,1152]{2,1,0:T(2,128)(2,1)}, ...) | async-done | bytes 737296 | tf_op jit(solution)/shard_map/psum | solution.py:11
  112.3 0.0 copy-start.1
  112.3 2.0 slice_convert_fusion.1
  114.3 1.8 slice_convert_fusion.5
  116.2 0.0 copy-done.1
  116.3 10.6 %fusion.2 = (f32[32,1152]{1,0:T(8,128)S(1)}, f32[32,1152]{1,0:T(8,128)S(1)}, f32[32,1152]{1,0:T(8,128)S(1)}, f32[32,1152]{1,0:T(8,128)S(1)}, f32[32,1152]{1,0:T(...) fusion(f32[40,1152]{1,0:T(8,128)S(1)} %bitcast.70, ...), kind=kLoop, calls=%fused_computation.18 | loop fusion | flops 61636608 | bytes 8557568 | tf_op jit(solution)/shard_map/reduce_sum | solution.py:26
  126.9 0.0 copy-start.4
  126.9 0.1 stack.51
  127.0 0.1 stack.52
  127.1 0.1 stack.55
  127.2 0.1 stack.56
  127.3 0.1 stack.59
  127.5 0.1 stack.60
  127.6 0.1 stack.63
  127.7 0.1 stack.64
  127.8 1.0 pad_maximum_fusion
  128.8 1.0 pad_maximum_fusion.1
  129.8 1.0 pad_maximum_fusion.2
  130.8 1.0 pad_maximum_fusion.3
  131.8 0.0 all-reduce.9.cloned.1.call-update
  131.8 0.0 copy-done.4
  131.8 0.6 dynamic-slice
  133.0 225.6 %all-reduce.9.cloned.1.call-done = (f32[32,2,1152]{2,1,0:T(2,128)}, f32[32,2,1152]{2,1,0:T(2,128)}, f32[32,2,1152]{2,1,0:T(2,128)}, f32[32,2,1152]{2,1,0:T(2,128)}) async-done(((f32[32,2,1152]{2,1,0:T(2,128)}, f32[32,2,1152]{2,1,0:T(2,128)}, f32[32,2,1152]{2,1,0:T(2,128)}, f32[32,2,1152]{2,1,0:T(2,128)}), (f32[32,2,1152]{2,1,0:T(2,128)}, f32[32,2,1152]{2,1,0:T(2,128)}, f32[32,2,1152]{2,1,0:T(2,128)}, ...) | async-done | bytes 1179664
  358.6 0.9 dynamic-slice_bitcast_fusion
  359.6 0.9 dynamic-slice_bitcast_fusion.1
  360.5 0.9 dynamic-slice_bitcast_fusion.2
  361.5 0.9 dynamic-slice_bitcast_fusion.3
  362.4 0.7 pad_maximum_fusion.4
  (9 shorter events, 0.1 us)
Async XLA Ops:
  6.5 29.6 %copy-start = (f32[8,32]{1,0:T(8,128)S(1)}, f32[8,32]{1,0:T(8,128)}, u32[]{:S(2)}) copy-start(f32[8,32]{1,0:T(8,128)} %param.8) | copy-start | bytes 3076
  6.5 105.7 %all-reduce.11.cloned.1.call-start = ((), (), s32[]{:S(2)}) async-start(), calls=%async_computation.1 | async-start | bytes 1474560 | tf_op jit(solution)/shard_map/psum | solution.py:11
  20.9 15.2 %copy-start.2 = (s32[1,40]{1,0:T(1,128)S(1)}, s32[1,40]{1,0:T(1,128)}, u32[]{:S(2)}) copy-start(s32[1,40]{1,0:T(1,128)} %param.10) | copy-start | bytes 484
  21.0 15.2 %copy-start.3 = (s32[1,40]{1,0:T(1,128)S(1)}, s32[1,40]{1,0:T(1,128)}, u32[]{:S(2)}) copy-start(s32[1,40]{1,0:T(1,128)} %param.9) | copy-start | bytes 484
  21.0 337.7 %all-reduce.9.cloned.1.call-start = ((), (), s32[]{:S(2)}) async-start(), calls=%async_computation | async-start | bytes 2359296
  112.3 4.0 %copy-start.1 = (bf16[40,32,1,1152]{3,2,1,0:T(2,128)(2,1)S(1)}, bf16[40,32,1,1152]{3,2,1,0:T(2,128)(2,1)}, u32[]{:S(2)}) copy-start(bf16[40,32,1,1152]{3,2,1,0:T(2,128)(2,1)} %get-tuple-element.27) | copy-start | bytes 8847364
  126.9 4.9 %copy-start.4 = (u32[256]{0:T(256)S(1)}, u32[256]{0:T(256)}, u32[]{:S(2)}) copy-start(u32[256]{0:T(256)} %constant.86) | copy-start | bytes 3076
Sparse Core Ops, SparseCore 0:
  21.1 91.1 all-reduce.10
  131.9 226.6 all-reduce.8
where the time goes:
time: 371 us; the launch traced here: 370 us
  waiting for transfers between devices  302 us (81%)
  between operations  24.5 us (7%)
  local copies, waits for them, and re-layouts  21.9 us (6%)
  other arithmetic  21.8 us (6%)
    unnamed x3, waiting for transfers between devices  226 us
    psum x1, waiting for transfers between devices, from_root(): return lax.psum(kept, axis)  75.9 us
    slice x1, local copies, waits for them, and re-layouts, predicted(): real_panel = block[:, :, 0, :].astype(jnp.float32)  15.1 us
    reduce_sum x1, other arithmetic, predicted(): jnp.sum(scale * (real_trace * real_panel - imag_trace * imag_panel), axis=0)  10.6 us
  transfers between devices with their start and end apart: 2, of which 2 were waited for; matrix products, arithmetic and copies ran while one was open for 4% of the time, Pallas kernels for 0%

commit v1 on v0

v1 whole, which is shorter than its diff:
```python
import functools

import jax
import jax.numpy as jnp
from jax import lax
from jax.experimental import pallas as pl
from jax.experimental.pallas import tpu as pltpu
from jax.sharding import PartitionSpec as P

F32 = jnp.float32
BF16 = jnp.bfloat16
MESH = pl.DeviceIdType.MESH

F = 1152
R = 32
K = 40
S = 4
N_OUT = 8
CH = K // N_OUT
TILE = 128
MAIN = 1024
LAST = F - MAIN
FB = 36
UNROLL = 8

OUT_OFF = ((1, 1), (3, 1), (2, 1), (1, 0), (3, 0), (2, 0), (0, 1))
Z_OFF = (4, 3, 5, 2, 6, 1, 7)


def kernel(
    panels, shots, table, dest, level, order, out,
    pm, pt, pmf, ptf, wt, recv1, gath, tr, trs, u, v, ts, cs, cr, yr, zr, fs,
    psem, ptsem, own_sem, s1, r1, s2, r2, sc, rc, sy, ry, sz, rz,
):
    o = lax.axis_index("out")
    a = lax.axis_index("ap")
    x, yh = o // 2, o % 2
    z, yl, c = a // 4, (a // 2) % 2, a % 2

    pm_copy = pltpu.make_async_copy(panels.at[:, :, :, pl.ds(0, MAIN)], pm, psem)
    pm_copy.start()
    pt_copies = []
    for r in range(R):
        cp = pltpu.make_async_copy(
            panels.at[:, r, :, pl.ds(MAIN, LAST)], pt.at[:, :, pl.ds(r * LAST, LAST)], ptsem.at[r]
        )
        cp.start()
        pt_copies.append(cp)
    own = pltpu.make_async_copy(shots.at[:, pl.ds(o * CH, CH)], recv1.at[pl.ds(2 * o, 2)], own_sem)
    own.start()

    out_ids = [((lax.rem(x + dx, 4) * 2 + lax.rem(yh + dy, 2)), a) for dx, dy in OUT_OFF]
    core_id = (o, (z * 2 + yl) * 2 + 1 - c)
    y_id = (o, (z * 2 + 1 - yl) * 2 + c)
    z_at = [lax.rem(z + dz, 8) for dz in Z_OFF]
    z_ids = [(o, (zz * 2 + yl) * 2 + c) for zz in z_at]

    barrier = pltpu.get_barrier_semaphore()
    peers = out_ids + [core_id, y_id] + z_ids
    for peer in peers:
        pl.semaphore_signal(barrier, inc=1, device_id=peer, device_id_type=MESH)
    pl.semaphore_wait(barrier, len(peers))

    first = []
    for i, peer in enumerate(out_ids):
        cp = pltpu.make_async_remote_copy(
            src_ref=shots.at[:, pl.ds(peer[0] * CH, CH)], dst_ref=recv1.at[pl.ds(2 * o, 2)],
            send_sem=s1.at[i], recv_sem=r1.at[i], device_id=peer, device_id_type=MESH,
        )
        cp.start()
        first.append(cp)

    def fill(l, _):
        for r in range(R):
            wt[l, :, r * LAST:(r + 1) * LAST] = jnp.full((2, LAST), table[l, r], F32)
        return 0

    lax.fori_loop(0, 8, fill, 0)
    pm_copy.wait()
    for cp in pt_copies:
        cp.wait()

    def weigh(k, _):
        lev = level[0, k]
        live = jnp.where(dest[0, k] >= 0, 1.0, 0.0).astype(F32)
        for r in range(R):
            pmf[k, r] = pm[k, r].astype(F32) * (table[lev, r] * live)
        ptf[k] = pt[k].astype(F32) * (wt[lev] * live)
        return 0

    lax.fori_loop(0, K, weigh, 0)

    own.wait()
    for cp in first:
        cp.wait_recv()

    second = []
    mine = pl.ds(o * CH, CH)
    for s in range(S):
        gath[s, mine] = recv1[order[s]]
        copies = []
        for i, peer in enumerate(out_ids):
            cp = pltpu.make_async_remote_copy(
                src_ref=gath.at[s, mine], dst_ref=gath.at[s, mine],
                send_sem=s2.at[s, i], recv_sem=r2.at[s, i], device_id=peer, device_id_type=MESH,
            )
            cp.start()
            copies.append(cp)
        second.append(copies)

    zero = jnp.zeros((2, 512), F32)

    def traces(s):
        for cp in second[s]:
            cp.wait_recv()

        def body(k, _):
            t = gath[s, k].astype(F32)
            tr[k, :, 0:F] = t
            for i in range(3):
                tr[k, :, F + i * LAST:F + (i + 1) * LAST] = t[:, MAIN:]
            return 0

        lax.fori_loop(0, K, body, 0, unroll=4)

        def swap(k, _):
            trs[k, 0:1] = tr[k, 1:2]
            trs[k, 1:2] = tr[k, 0:1]
            return 0

        lax.fori_loop(0, K, swap, 0, unroll=4)

    def group(load, col, store):
        def body(k, acc):
            t, w = tr[k, :, col:col + 512], trs[k, :, col:col + 512]
            new = []
            for g in range(8):
                p = load(k, g)
                new.append(acc[2 * g] + t * p)
                new.append(acc[2 * g + 1] + w * p)
            return tuple(new)

        acc = lax.fori_loop(0, K, body, (zero,) * 16, unroll=UNROLL)
        for g in range(8):
            store(g, acc[2 * g], acc[2 * g + 1])

    def products(s, parts):
        for part in parts:
            if part < 8:
                half, first_r = part % 2, (part // 2) * 8
                cols = slice(half * 512, half * 512 + 512)

                def load(k, g, first_r=first_r, cols=cols):
                    return pmf[k, first_r + g, :, cols]

                def store(g, p, q, first_r=first_r, cols=cols):
                    u[s, first_r + g, :, cols] = p
                    v[s, first_r + g, :, cols] = q

                group(load, half * 512, store)
            else:

                def load(k, g):
                    return ptf[k, :, g * 512:g * 512 + 512]

                def store(g, p, q):
                    for i in range(4):
                        u[s, g * 4 + i, :, MAIN:F] = p[:, i * LAST:(i + 1) * LAST]
                        v[s, g * 4 + i, :, MAIN:F] = q[:, i * LAST:(i + 1) * LAST]

                group(load, MAIN, store)

    def turn(h):
        even = lax.broadcasted_iota(jnp.int32, (64, TILE), 0) % 2 == 0
        for ft in range(F // TILE):
            rows = []
            for s in (2 * h, 2 * h + 1):
                cols = slice(ft * TILE, (ft + 1) * TILE)
                p = u[s, :, :, cols].reshape(64, TILE)
                q = v[s, :, :, cols].reshape(64, TILE)
                rows.append(jnp.where(even, p - pltpu.roll(p, 63, 0), q + pltpu.roll(q, 1, 0)))
            ts[ft * TILE:(ft + 1) * TILE] = jnp.concatenate(rows, axis=0).T
        for b in range(32):
            cs[h, b % 2, (b // 2) % 2, b // 4] = ts[b * FB:(b + 1) * FB]

    def remote(src, dst, send, recv, peer):
        cp = pltpu.make_async_remote_copy(
            src_ref=src, dst_ref=dst, send_sem=send, recv_sem=recv, device_id=peer, device_id_type=MESH
        )
        cp.start()
        return cp

    def core_start(h):
        return remote(cs.at[h, 1 - c], cr.at[h], sc.at[h], rc.at[h], core_id)

    def y_start(h, cp):
        cp.wait_recv()
        cr[h] = cr[h] + cs[h, c]
        return remote(cr.at[h, 1 - yl], yr.at[h], sy.at[h], ry.at[h], y_id)

    def z_start(h, cp):
        cp.wait_recv()
        yr[h] = yr[h] + cr[h, yl]
        return [
            remote(yr.at[h, z_at[i]], zr.at[h, i], sz.at[h, i], rz.at[h, i], z_ids[i]) for i in range(7)
        ]

    def finish(h, copies):
        for cp in copies:
            cp.wait_recv()
        total = yr[h, z]
        for i in range(7):
            total = total + zr[h, i]
        fs[h, 0:FB] = total
        flat = fs[h].T
        for i in range(2):
            out[2 * h + i] = flat[64 * i:64 * i + 64, 0:FB]

    for s in (0, 1):
        traces(s)
        products(s, range(9))
    turn(0)
    core0 = core_start(0)
    traces(2)
    products(2, range(5))
    y0 = y_start(0, core0)
    products(2, range(5, 9))
    traces(3)
    products(3, range(9))
    turn(1)
    core1 = core_start(1)
    z0 = z_start(0, y0)
    y1 = y_start(1, core1)
    z1 = z_start(1, y1)
    finish(0, z0)
    finish(1, z1)

    for cp in first + [cp for copies in second for cp in copies] + [core0, y0, core1, y1] + z0 + z1:
        cp.wait_send()


def on_device(panels, shot_data, taper_table, destination, taper_level, shot_order):
    vmem = pltpu.VMEM
    dma = pltpu.SemaphoreType.DMA
    hbm = pl.BlockSpec(memory_space=pl.ANY)
    smem = pl.BlockSpec(memory_space=pltpu.SMEM)
    result = pl.pallas_call(
        kernel,
        out_shape=jax.ShapeDtypeStruct((S, 2 * R, FB), F32),
        in_specs=[hbm, hbm, smem, smem, smem, smem],
        out_specs=pl.BlockSpec(memory_space=vmem),
        scratch_shapes=[
            vmem((K, R, 2, MAIN), BF16),
            vmem((K, 2, R * LAST), BF16),
            vmem((K, R, 2, MAIN), F32),
            vmem((K, 2, R * LAST), F32),
            vmem((8, 2, R * LAST), F32),
            vmem((2 * N_OUT, CH, 2, F), BF16),
            vmem((S, K, 2, F), BF16),
            vmem((K, 2, F + 3 * LAST), F32),
            vmem((K, 2, F + 3 * LAST), F32),
            vmem((S, R, 2, F), F32),
            vmem((S, R, 2, F), F32),
            vmem((F, TILE), F32),
            vmem((2, 2, 2, 8, FB, TILE), F32),
            vmem((2, 2, 8, FB, TILE), F32),
            vmem((2, 8, FB, TILE), F32),
            vmem((2, 7, FB, TILE), F32),
            vmem((2, TILE, TILE), F32),
            dma, dma((R,)), dma,
            dma((7,)), dma((7,)), dma((S, 7)), dma((S, 7)),
            dma((2,)), dma((2,)), dma((2,)), dma((2,)), dma((2, 7)), dma((2, 7)),
        ],
        compiler_params=pltpu.CompilerParams(
            collective_id=0, has_side_effects=True, vmem_limit_bytes=48 * 2**20
        ),
        name="multiples",
    )(panels, shot_data, taper_table, destination, taper_level, shot_order)
    return result.reshape(S, R, 2, FB)


def solution(mesh):
    placed = (
        P("ap", "out", None, None),
        P("out", "ap", None, None),
        P(),
        P("out", "ap"),
        P("out", "ap"),
        P(),
    )
    return jax.shard_map(
        on_device, mesh=mesh, in_specs=placed, out_specs=P(None, "out", None, "ap"), check_vma=False
    )
```

time: 371 us -> 50.9 us (0.14)
  waiting for transfers between devices: 302 us -> 0 us
  Pallas kernels: 0 us -> 46.5 us
  between operations: 24.5 us -> 0.01 us
  other arithmetic: 21.8 us -> 0 us
  local copies, waits for them, and re-layouts: 21.9 us -> 4.3 us
    unnamed x3 -> x0, waiting for transfers between devices: 226 us -> none
    psum x1 -> x0, waiting for transfers between devices: 75.9 us -> none  [from_root(): return lax.psum(kept, axis)]
    pallas_call x0 -> x1, Pallas kernels: none -> 46.5 us  [on_device(): pl.pallas_call(kernel, out_shape=jax.ShapeDtypeStruct((S, 2 * R, FB), F32...]
    slice x2 -> x0, local copies, waits for them, and re-layouts: 16.6 us -> none  [the longest x1 15.1 us: predicted(): real_panel = block[:, :, 0, :].astype(jnp.float32)]
    reduce_sum x1 -> x0, other arithmetic: 10.6 us -> none  [predicted(): jnp.sum(scale * (real_trace * real_panel - imag_trace * imag_panel), axis=0)]
    another operation x5 -> x0, other arithmetic: 4.69 us -> none  [the longest x4 3.96 us: predicted(): return jnp.stack([real_part, imag_part], axis=1)]
    another operation x12 -> x0, local copies, waits for them, and re-layouts: 4.57 us -> none  [the longest x4 3.74 us: on_device(): return jnp.stack(totals, axis=0)]
    mul x2 -> x0, other arithmetic: 3.8 us -> none  [predicted(): real_trace * real_panel - imag_trace * imag_panel]
  transfers between devices with their start and end apart: 2 -> 0, of which waited for: 2 -> 0; matrix products, arithmetic and copies ran while one was open for 4% -> 0% of each run, Pallas kernels for 0% -> 0%
where the time goes in v1:
time: 50.9 us; the launch traced here: 50.8 us
  Pallas kernels  46.5 us (91%)
  local copies, waits for them, and re-layouts  4.3 us (8%)
    pallas_call x1, Pallas kernels, on_device(): pl.pallas_call(kernel, out_shape=jax.ShapeDtypeStruct((S, 2 * R, FB), F32...  46.5 us
    unnamed x11, local copies, waits for them, and re-layouts  4.3 us

profile of v1, /device:TPU:1, one launch (start us, length us, event | category | flops | bytes accessed | tf_op | source)
XLA Modules:
  0.0 50.8 jit_solution(9127846307604977324)
XLA Ops:
  0.0 0.0 copy-start
  0.0 1.0 %copy-done = bf16[2,40,2,1152]{3,2,1,0:T(2,128)(2,1)S(1)} copy-done((bf16[2,40,2,1152]{3,2,1,0:T(2,128)(2,1)S(1)}, bf16[2,40,2,1152]{3,2,1,0:T(2,128)(2,1)}, u32[]{:S(2)}) %copy-start) | copy-done | bytes 368664
  1.0 0.0 copy-start.1
  1.0 0.7 %copy-done.1 = f32[8,32]{1,0:T(8,128)S(1)} copy-done((f32[8,32]{1,0:T(8,128)S(1)}, f32[8,32]{1,0:T(8,128)}, u32[]{:S(2)}) %copy-start.1) | copy-done | bytes 1048
  1.7 0.0 copy-start.2
  1.7 0.7 %copy-done.2 = s32[1,40]{1,0:T(1,128)S(1)} copy-done((s32[1,40]{1,0:T(1,128)S(1)}, s32[1,40]{1,0:T(1,128)}, u32[]{:S(2)}) %copy-start.2) | copy-done | bytes 184
  2.3 0.0 copy-start.3
  2.3 0.7 %copy-done.3 = s32[1,40]{1,0:T(1,128)S(1)} copy-done((s32[1,40]{1,0:T(1,128)S(1)}, s32[1,40]{1,0:T(1,128)}, u32[]{:S(2)}) %copy-start.3) | copy-done | bytes 184
  3.0 0.0 copy-start.4
  3.0 0.7 %copy-done.4 = s32[4]{0:T(128)S(1)} copy-done((s32[4]{0:T(128)S(1)}, s32[4]{0:T(128)}, u32[]{:S(2)}) %copy-start.4) | copy-done | bytes 40
  3.6 46.5 %multiples.1 = f32[4,64,36]{2,1,0:T(8,128)S(1)} custom-call(bf16[40,32,2,1152]{3,2,1,0:T(2,128)(2,1)} %panels.1, bf16[2,40,2,1152]{3,2,1,0:T(2,128)(2,1)S(1)} %copy-done, f32[8,32]{1,0:T(8,128)S(1)} %copy-done.1, s32[1,40]{1,0:T(1,128)S(1)} %copy-done.2, s32[1,40]{1,0:T(1,128)S(1)} %copy-done.3, s32[4]{0:T(128)S(1)} %copy-done.4), custom_call_target="tpu_custom_call" | custom-call | tf_op jit(solution)/shard_map/multiples/pallas_call | solution.py:247
  50.1 0.7 %copy.8 = f32[4,32,2,36]{3,2,1,0:T(2,128)} copy(f32[4,32,2,36]{3,2,1,0:T(2,128)S(1)} %bitcast.1) | data formatting | bytes 73728
Async XLA Ops:
  0.0 1.0 %copy-start = (bf16[2,40,2,1152]{3,2,1,0:T(2,128)(2,1)S(1)}, bf16[2,40,2,1152]{3,2,1,0:T(2,128)(2,1)}, u32[]{:S(2)}) copy-start(bf16[2,40,2,1152]{3,2,1,0:T(2,128)(2,1)} %shots.1) | copy-start | bytes 1105924
  1.0 0.7 %copy-start.1 = (f32[8,32]{1,0:T(8,128)S(1)}, f32[8,32]{1,0:T(8,128)}, u32[]{:S(2)}) copy-start(f32[8,32]{1,0:T(8,128)} %table.1) | copy-start | bytes 3076
  1.7 0.7 %copy-start.2 = (s32[1,40]{1,0:T(1,128)S(1)}, s32[1,40]{1,0:T(1,128)}, u32[]{:S(2)}) copy-start(s32[1,40]{1,0:T(1,128)} %dest.1) | copy-start | bytes 484
  2.3 0.7 %copy-start.3 = (s32[1,40]{1,0:T(1,128)S(1)}, s32[1,40]{1,0:T(1,128)}, u32[]{:S(2)}) copy-start(s32[1,40]{1,0:T(1,128)} %level.1) | copy-start | bytes 484
  3.0 0.7 %copy-start.4 = (s32[4]{0:T(128)S(1)}, s32[4]{0:T(128)}, u32[]{:S(2)}) copy-start(s32[4]{0:T(128)} %order.1) | copy-start | bytes 52

commit v2 on v0

v2 whole, which is shorter than its diff:
```python
import functools

import jax
import jax.numpy as jnp
from jax import lax
from jax.experimental import pallas as pl
from jax.experimental.pallas import tpu as pltpu
from jax.sharding import PartitionSpec as P

F32 = jnp.float32
BF16 = jnp.bfloat16
MESH = pl.DeviceIdType.MESH

F = 1152
R = 32
K = 40
S = 4
N_OUT = 8
CH = K // N_OUT
TILE = 128
MAIN = 1024
LAST = F - MAIN
FB = 36
HB = FB // 2
UNROLL = 8

OUT_OFF = ((1, 1), (3, 1), (2, 1), (1, 0), (3, 0), (2, 0), (0, 1))
X_OFF = (2, 1, 3)
WAYS = ("all", "all", "all", "all")
Z_OFF = (4, 3, 5, 2, 6, 1, 7)


def kernel(
    panels, shots, table_hbm, dest_hbm, level_hbm, order_hbm, out,
    table, dest, level, order,
    pm, pt, tmp, tmpl, pmf, ptf, wt, recv1, gath, tr, xs, xl, ts, cs, cr, ys, yo, yr, zs, zr, fs,
    small_sem, psem, ptsem, own_sem, s1, r1, s2, r2, s2x, r2x, sc, rc, sy, ry, sz, rz,
):
    o = lax.axis_index("out")
    a = lax.axis_index("ap")
    x, yh = o // 2, o % 2
    z, yl, c = a // 4, (a // 2) % 2, a % 2

    small = []
    for i, (src, dst) in enumerate(((table_hbm, table), (dest_hbm, dest), (level_hbm, level), (order_hbm, order))):
        cp = pltpu.make_async_copy(src, dst, small_sem.at[i])
        cp.start()
        small.append(cp)

    pm_copy = pltpu.make_async_copy(panels.at[:, :, :, pl.ds(0, MAIN)], pm, psem)
    pm_copy.start()
    pt_copies = []
    for r in range(R):
        cp = pltpu.make_async_copy(
            panels.at[:, r, :, pl.ds(MAIN, LAST)], pt.at[:, :, pl.ds(r * LAST, LAST)], ptsem.at[r]
        )
        cp.start()
        pt_copies.append(cp)
    own = pltpu.make_async_copy(shots.at[:, pl.ds(o * CH, CH)], recv1.at[pl.ds(2 * o, 2)], own_sem)
    own.start()

    out_ids = [((lax.rem(x + dx, 4) * 2 + lax.rem(yh + dy, 2)), a) for dx, dy in OUT_OFF]
    x_ids = [(lax.rem(x + dx, 4) * 2 + yh, a) for dx in X_OFF]
    row_id = (x * 2 + 1 - yh, a)
    core_id = (o, (z * 2 + yl) * 2 + 1 - c)
    y_id = (o, (z * 2 + 1 - yl) * 2 + c)
    z_at = [lax.rem(z + dz, 8) for dz in Z_OFF]
    z_ids = [(o, (zz * 2 + yl) * 2 + c) for zz in z_at]

    barrier = pltpu.get_barrier_semaphore()
    peers = out_ids + [core_id, y_id] + z_ids
    for peer in peers:
        pl.semaphore_signal(barrier, inc=1, device_id=peer, device_id_type=MESH)
    pl.semaphore_wait(barrier, len(peers))

    first = []
    for i, peer in enumerate(out_ids):
        cp = pltpu.make_async_remote_copy(
            src_ref=shots.at[:, pl.ds(peer[0] * CH, CH)], dst_ref=recv1.at[pl.ds(2 * o, 2)],
            send_sem=s1.at[i], recv_sem=r1.at[i], device_id=peer, device_id_type=MESH,
        )
        cp.start()
        first.append(cp)

    for cp in small:
        cp.wait()

    def fill(l, _):
        for r in range(R):
            wt[l, :, r * LAST:(r + 1) * LAST] = jnp.full((1, LAST), table[l, r], F32)
        return 0

    lax.fori_loop(0, 8, fill, 0)
    pm_copy.wait()
    for cp in pt_copies:
        cp.wait()

    def weigh(k, _):
        lev = level[0, k]
        live = jnp.where(dest[0, k] >= 0, 1.0, 0.0).astype(F32)
        for r in range(R):
            tmp[r] = pm[k, r].astype(F32)
        tmpl[...] = pt[k].astype(F32)
        for r in range(R):
            weight = table[lev, r] * live
            re = tmp[r, 0:1] * weight
            im = tmp[r, 1:2] * weight
            pmf[k, 0, r] = re
            pmf[k, 1, r] = im - re
            pmf[k, 2, r] = re + im
        weight = wt[lev] * live
        re = tmpl[0:1] * weight
        im = tmpl[1:2] * weight
        for i, value in enumerate((re, im - re, re + im)):
            ptf[k, i] = value.reshape(R, LAST)
        return 0

    lax.fori_loop(0, K, weigh, 0)

    own.wait()
    for cp in first:
        cp.wait_recv()

    def remote(src, dst, send, recv, peer):
        cp = pltpu.make_async_remote_copy(
            src_ref=src, dst_ref=dst, send_sem=send, recv_sem=recv, device_id=peer, device_id_type=MESH
        )
        cp.start()
        return cp

    for s in range(S):
        gath[s, x, yh] = recv1[order[s]]

    def spread(s, peers, to, send, recv):
        part = gath.at[(s,) + to]
        return [remote(part, part, send.at[s, i], recv.at[s, i], peer) for i, peer in enumerate(peers)]

    near = []
    for s, way in enumerate(WAYS):
        if way == "all":
            near.append(spread(s, out_ids, (x, yh), s2, r2))
        elif way == "y":
            near.append(spread(s, [row_id], (x, yh), s2, r2))
        else:
            near.append(spread(s, x_ids, (x, yh), s2, r2))
    second = []
    for s, way in enumerate(WAYS):
        if way == "all":
            second.append(near[s])
            continue
        for cp in near[s]:
            cp.wait_recv()
        if way == "y":
            second.append(spread(s, x_ids, (x,), s2x, r2x))
        else:
            second.append(spread(s, [row_id], (slice(None), yh), s2x, r2x))
    rows = [cp for s, way in enumerate(WAYS) if way != "all" for cp in near[s]]

    def traces(s):
        for cp in second[s]:
            cp.wait_recv()

        def body(k, _):
            tr[k] = gath[s, k // (2 * CH), (k // CH) % 2, k % CH].astype(F32)
            return 0

        lax.fori_loop(0, K, body, 0, unroll=4)

    def sums(width, load, cols, count, shape):
        def body(k, acc):
            a, b = tr[k, 0:1, cols], tr[k, 1:2, cols]
            t = (a + b, a, b)
            return tuple(acc[3 * g + i] + t[i] * load(k, i, g) for g in range(count) for i in range(3))

        acc = lax.fori_loop(0, K, body, (jnp.zeros(shape, F32),) * (3 * count), unroll=UNROLL)
        return [(acc[3 * g] - acc[3 * g + 2], acc[3 * g] + acc[3 * g + 1]) for g in range(count)]

    def products(s, parts):
        for part in parts:
            if part < 4:
                pairs = sums(
                    MAIN, lambda k, i, g, part=part: pmf[k, i, part * 8 + g], slice(0, MAIN), 8, (1, MAIN)
                )
                for g, (re, im) in enumerate(pairs):
                    r = part * 8 + g
                    xs[s, 2 * r:2 * r + 1] = re
                    xs[s, 2 * r + 1:2 * r + 2] = im
            else:
                pairs = sums(
                    LAST, lambda k, i, g: ptf[k, i, g * 8:g * 8 + 8], slice(MAIN, F), 4, (8, LAST)
                )
                for g, (re, im) in enumerate(pairs):
                    xl[s, pl.ds(g * 16, 8, stride=2)] = re
                    xl[s, pl.ds(g * 16 + 1, 8, stride=2)] = im

    def turn(s):
        copies = []
        tiles = [xl[s] if ft == 8 else xs[s, :, ft * TILE:(ft + 1) * TILE] for ft in range(F // TILE)]
        turned = [pltpu.roll(tile, TILE // 2, 1) for tile in tiles[4:]]
        low = lax.broadcasted_iota(jnp.int32, (2 * R, TILE), 1) < TILE // 2
        for j in range(5):
            upper = jnp.where(low, turned[j], turned[min(j + 1, 4)])
            ts[j * TILE:(j + 1) * TILE] = jnp.concatenate([tiles[j], upper], axis=0).T
            if j in (2, 4):
                part = j // 4
                for b in range(part * 8, part * 8 + 8):
                    cs[s, b % 2, (b // 2) % 2, b // 4] = ts[b * FB:(b + 1) * FB]
                zz = pl.ds(2 * part, 2)
                copies.append(
                    remote(cs.at[s, 1 - c, :, zz], cr.at[s, :, zz], sc.at[s, part], rc.at[s, part], core_id)
                )
        return copies

    def y_start(s, copies):
        for cp in copies:
            cp.wait_recv()
        ys[s] = cs[s, c, 1 - yl] + cr[s, 1 - yl]
        sent = remote(ys.at[s], yr.at[s], sy.at[s], ry.at[s], y_id)
        yo[s] = cs[s, c, yl] + cr[s, yl]
        return [sent]

    def z_start(s, copies):
        copies[0].wait_recv()
        low = lax.broadcasted_iota(jnp.int32, (HB, TILE), 1) < TILE // 2
        for zz in range(4):
            first_half = yo[s, zz, 0:HB] + yr[s, zz, 0:HB]
            second_half = yo[s, zz, HB:FB] + yr[s, zz, HB:FB]
            zs[s, zz] = jnp.where(low, first_half, pltpu.roll(second_half, TILE // 2, 1))
            zs[s, zz + 4] = jnp.where(low, pltpu.roll(first_half, TILE // 2, 1), second_half)
        return [remote(zs.at[s, z_at[i]], zr.at[s, i], sz.at[s, i], rz.at[s, i], z_ids[i]) for i in range(7)]

    def finish(s, copies):
        for cp in copies:
            cp.wait_recv()
        total = zs[s, z]
        for i in range(7):
            total = total + zr[s, i]
        fs[s, 0:HB] = total
        flat = fs[s].T
        out[s, :, 0:HB] = flat[0:2 * R, 0:HB]
        out[s, :, HB:FB] = flat[2 * R:, 0:HB]

    traces(0)
    products(0, range(5))
    core = [turn(0)]
    traces(1)
    products(1, range(3))
    y = [y_start(0, core[0])]
    products(1, range(3, 5))
    core.append(turn(1))
    traces(2)
    products(2, range(3))
    y.append(y_start(1, core[1]))
    products(2, range(3, 5))
    core.append(turn(2))
    traces(3)
    products(3, range(3))
    y.append(y_start(2, core[2]))
    zc = [z_start(0, y[0])]
    products(3, range(3, 5))
    core.append(turn(3))
    zc.append(z_start(1, y[1]))
    y.append(y_start(3, core[3]))
    zc.append(z_start(2, y[2]))
    zc.append(z_start(3, y[3]))
    for s in range(S):
        finish(s, zc[s])

    for cp in first + rows + [cp for copies in second + core + y + zc for cp in copies]:
        cp.wait_send()


def on_device(panels, shot_data, taper_table, destination, taper_level, shot_order):
    vmem = pltpu.VMEM
    dma = pltpu.SemaphoreType.DMA
    hbm = pl.BlockSpec(memory_space=pltpu.HBM)
    result = pl.pallas_call(
        kernel,
        out_shape=jax.ShapeDtypeStruct((S, 2 * R, FB), F32),
        in_specs=[hbm] * 6,
        out_specs=pl.BlockSpec(memory_space=vmem),
        scratch_shapes=[
            pltpu.SMEM((8, R), F32),
            pltpu.SMEM((1, K), jnp.int32),
            pltpu.SMEM((1, K), jnp.int32),
            pltpu.SMEM((S,), jnp.int32),
            vmem((K, R, 2, MAIN), BF16),
            vmem((K, 2, R * LAST), BF16),
            vmem((R, 2, MAIN), F32),
            vmem((2, R * LAST), F32),
            vmem((K, 3, R, 1, MAIN), F32),
            vmem((K, 3, R, LAST), F32),
            vmem((8, 1, R * LAST), F32),
            vmem((2 * N_OUT, CH, 2, F), BF16),
            vmem((S, 4, 2, CH, 2, F), BF16),
            vmem((K, 2, F), F32),
            vmem((S, 2 * R, MAIN), F32),
            vmem((S, 2 * R, LAST), F32),
            vmem((5 * TILE, TILE), F32),
            vmem((S, 2, 2, 4, FB, TILE), F32),
            vmem((S, 2, 4, FB, TILE), F32),
            vmem((S, 4, FB, TILE), F32),
            vmem((S, 4, FB, TILE), F32),
            vmem((S, 4, FB, TILE), F32),
            vmem((S, 8, HB, TILE), F32),
            vmem((S, 7, HB, TILE), F32),
            vmem((S, TILE, TILE), F32),
            dma((4,)), dma, dma((R,)), dma,
            dma((7,)), dma((7,)), dma((S, 7)), dma((S, 7)), dma((S, 3)), dma((S, 3)),
            dma((S, 2)), dma((S, 2)), dma((S,)), dma((S,)), dma((S, 7)), dma((S, 7)),
        ],
        compiler_params=pltpu.CompilerParams(
            collective_id=0, has_side_effects=True, vmem_limit_bytes=48 * 2**20
        ),
        name="multiples",
    )(*[pltpu.with_memory_space_constraint(v, pltpu.HBM) for v in (panels, shot_data, taper_table, destination, taper_level, shot_order)])
    return result.reshape(S, R, 2, FB)


def solution(mesh):
    placed = (
        P("ap", "out", None, None),
        P("out", "ap", None, None),
        P(),
        P("out", "ap"),
        P("out", "ap"),
        P(),
    )
    return jax.shard_map(
        on_device, mesh=mesh, in_specs=placed, out_specs=P(None, "out", None, "ap"), check_vma=False
    )
```

time: 371 us -> 43.6 us (0.12)
  waiting for transfers between devices: 302 us -> 0 us
  Pallas kernels: 0 us -> 42.9 us
  between operations: 24.5 us -> 0.01 us
  other arithmetic: 21.8 us -> 0 us
  local copies, waits for them, and re-layouts: 21.9 us -> 0.66 us
    unnamed x3 -> x0, waiting for transfers between devices: 226 us -> none
    psum x1 -> x0, waiting for transfers between devices: 75.9 us -> none  [from_root(): return lax.psum(kept, axis)]
    pallas_call x0 -> x1, Pallas kernels: none -> 42.9 us  [on_device(): pl.pallas_call(kernel, out_shape=jax.ShapeDtypeStruct((S, 2 * R, FB), F32...]
    slice x2 -> x0, local copies, waits for them, and re-layouts: 16.6 us -> none  [the longest x1 15.1 us: predicted(): real_panel = block[:, :, 0, :].astype(jnp.float32)]
    reduce_sum x1 -> x0, other arithmetic: 10.6 us -> none  [predicted(): jnp.sum(scale * (real_trace * real_panel - imag_trace * imag_panel), axis=0)]
    another operation x5 -> x0, other arithmetic: 4.69 us -> none  [the longest x4 3.96 us: predicted(): return jnp.stack([real_part, imag_part], axis=1)]
    another operation x12 -> x0, local copies, waits for them, and re-layouts: 4.57 us -> none  [the longest x4 3.74 us: on_device(): return jnp.stack(totals, axis=0)]
    mul x2 -> x0, other arithmetic: 3.8 us -> none  [predicted(): real_trace * real_panel - imag_trace * imag_panel]
  transfers between devices with their start and end apart: 2 -> 0, of which waited for: 2 -> 0; matrix products, arithmetic and copies ran while one was open for 4% -> 0% of each run, Pallas kernels for 0% -> 0%
where the time goes in v2:
time: 43.6 us
  Pallas kernels  42.9 us (98%)
  local copies, waits for them, and re-layouts  0.66 us (2%)
    pallas_call x1, Pallas kernels, on_device(): pl.pallas_call(kernel, out_shape=jax.ShapeDtypeStruct((S, 2 * R, FB), F32...  42.9 us

profile of v2, /device:TPU:1, one launch (start us, length us, event | category | flops | bytes accessed | tf_op | source)
XLA Modules:
  0.0 43.6 jit_solution(9690396678041747236)
XLA Ops:
  0.0 42.9 %multiples.1 = f32[4,64,36]{2,1,0:T(8,128)S(1)} custom-call(bf16[40,32,2,1152]{3,2,1,0:T(2,128)(2,1)} %panels.1, bf16[2,40,2,1152]{3,2,1,0:T(2,128)(2,1)} %shots.1, f32[8,32]{1,0:T(8,128)} %table_hbm.1, s32[1,40]{1,0:T(1,128)} %dest_hbm.1, s32[1,40]{1,0:T(1,128)} %level_hbm.1, s32[4]{0:T(128)} %order_hbm.1), custom_call_target="tpu_custom_call" | custom-call | tf_op jit(solution)/shard_map/multiples/pallas_call | solution.py:277
  42.9 0.7 %copy.8 = f32[4,32,2,36]{3,2,1,0:T(2,128)} copy(f32[4,32,2,36]{3,2,1,0:T(2,128)S(1)} %bitcast.1) | data formatting | bytes 73728

commit v3 on v2

--- a/solution.py
+++ b/solution.py
@@ -22,11 +22,9 @@
 LAST = F - MAIN
 FB = 36
 HB = FB // 2
-UNROLL = 8
+UNROLL = 20
 
 OUT_OFF = ((1, 1), (3, 1), (2, 1), (1, 0), (3, 0), (2, 0), (0, 1))
-X_OFF = (2, 1, 3)
-WAYS = ("all", "all", "all", "all")
 Z_OFF = (4, 3, 5, 2, 6, 1, 7)
 
 
@@ -34,7 +32,7 @@
     panels, shots, table_hbm, dest_hbm, level_hbm, order_hbm, out,
     table, dest, level, order,
     pm, pt, tmp, tmpl, pmf, ptf, wt, recv1, gath, tr, xs, xl, ts, cs, cr, ys, yo, yr, zs, zr, fs,
-    small_sem, psem, ptsem, own_sem, s1, r1, s2, r2, s2x, r2x, sc, rc, sy, ry, sz, rz,
+    small_sem, psem, ptsem, own_sem, s1, r1, s2, r2, sc, rc, sy, ry, sz, rz,
 ):
     o = lax.axis_index("out")
     a = lax.axis_index("ap")
@@ -60,8 +58,6 @@
     own.start()
 
     out_ids = [((lax.rem(x + dx, 4) * 2 + lax.rem(yh + dy, 2)), a) for dx, dy in OUT_OFF]
-    x_ids = [(lax.rem(x + dx, 4) * 2 + yh, a) for dx in X_OFF]
-    row_id = (x * 2 + 1 - yh, a)
     core_id = (o, (z * 2 + yl) * 2 + 1 - c)
     y_id = (o, (z * 2 + 1 - yl) * 2 + c)
     z_at = [lax.rem(z + dz, 8) for dz in Z_OFF]
@@ -135,63 +131,55 @@
         part = gath.at[(s,) + to]
         return [remote(part, part, send.at[s, i], recv.at[s, i], peer) for i, peer in enumerate(peers)]
 
-    near = []
-    for s, way in enumerate(WAYS):
-        if way == "all":
-            near.append(spread(s, out_ids, (x, yh), s2, r2))
-        elif way == "y":
-            near.append(spread(s, [row_id], (x, yh), s2, r2))
-        else:
-            near.append(spread(s, x_ids, (x, yh), s2, r2))
-    second = []
-    for s, way in enumerate(WAYS):
-        if way == "all":
-            second.append(near[s])
-            continue
-        for cp in near[s]:
+    second = [spread(s, out_ids, (x, yh), s2, r2) for s in range(S)]
+
+    whole = (K, UNROLL, lambda i: i)
+
+    def row(at):
+        return (K // 2, UNROLL // 2, lambda i: (i // CH) * (2 * CH) + at * CH + lax.rem(i, CH))
+
+    def traces(s, places, copies):
+        for cp in copies:
             cp.wait_recv()
-        if way == "y":
-            second.append(spread(s, x_ids, (x,), s2x, r2x))
-        else:
-            second.append(spread(s, [row_id], (slice(None), yh), s2x, r2x))
-    rows = [cp for s, way in enumerate(WAYS) if way != "all" for cp in near[s]]
-
-    def traces(s):
-        for cp in second[s]:
-            cp.wait_recv()
-
-        def body(k, _):
+        count, _, location = places
+
+        def body(i, _):
+            k = location(i)
             tr[k] = gath[s, k // (2 * CH), (k // CH) % 2, k % CH].astype(F32)
             return 0
 
-        lax.fori_loop(0, K, body, 0, unroll=4)
-
-    def sums(width, load, cols, count, shape):
-        def body(k, acc):
+        lax.fori_loop(0, count, body, 0, unroll=4)
+
+    def sums(places, load, cols, groups, shape):
+        count, unroll, location = places
+
+        def body(i, acc):
+            k = location(i)
             a, b = tr[k, 0:1, cols], tr[k, 1:2, cols]
             t = (a + b, a, b)
-            return tuple(acc[3 * g + i] + t[i] * load(k, i, g) for g in range(count) for i in range(3))
-
-        acc = lax.fori_loop(0, K, body, (jnp.zeros(shape, F32),) * (3 * count), unroll=UNROLL)
-        return [(acc[3 * g] - acc[3 * g + 2], acc[3 * g] + acc[3 * g + 1]) for g in range(count)]
-
-    def products(s, parts):
+            return tuple(acc[3 * g + n] + t[n] * load(k, n, g) for g in range(groups) for n in range(3))
+
+        acc = lax.fori_loop(0, count, body, (jnp.zeros(shape, F32),) * (3 * groups), unroll=unroll)
+        return [(acc[3 * g] - acc[3 * g + 2], acc[3 * g] + acc[3 * g + 1]) for g in range(groups)]
+
+    def products(s, places, parts, more=False):
         for part in parts:
             if part < 4:
                 pairs = sums(
-                    MAIN, lambda k, i, g, part=part: pmf[k, i, part * 8 + g], slice(0, MAIN), 8, (1, MAIN)
+                    places, lambda k, n, g, part=part: pmf[k, n, part * 8 + g], slice(0, MAIN), 8, (1, MAIN)
                 )
-                for g, (re, im) in enumerate(pairs):
-                    r = part * 8 + g
-                    xs[s, 2 * r:2 * r + 1] = re
-                    xs[s, 2 * r + 1:2 * r + 2] = im
+                for g, pair in enumerate(pairs):
+                    for n in range(2):
+                        at = pl.ds(2 * (part * 8 + g) + n, 1)
+                        xs[s, at] = xs[s, at] + pair[n] if more else pair[n]
             else:
                 pairs = sums(
-                    LAST, lambda k, i, g: ptf[k, i, g * 8:g * 8 + 8], slice(MAIN, F), 4, (8, LAST)
+                    places, lambda k, n, g: ptf[k, n, g * 8:g * 8 + 8], slice(MAIN, F), 4, (8, LAST)
                 )
-                for g, (re, im) in enumerate(pairs):
-                    xl[s, pl.ds(g * 16, 8, stride=2)] = re
-                    xl[s, pl.ds(g * 16 + 1, 8, stride=2)] = im
+                for g, pair in enumerate(pairs):
+                    for n in range(2):
+                        at = pl.ds(g * 16 + n, 8, stride=2)
+                        xl[s, at] = xl[s, at] + pair[n] if more else pair[n]
 
     def turn(s):
         copies = []
@@ -212,62 +200,81 @@
         return copies
 
     def y_start(s, copies):
-        for cp in copies:
-            cp.wait_recv()
-        ys[s] = cs[s, c, 1 - yl] + cr[s, 1 - yl]
-        sent = remote(ys.at[s], yr.at[s], sy.at[s], ry.at[s], y_id)
+        sent = []
+        for part in range(2):
+            copies[part].wait_recv()
+            two = pl.ds(2 * part, 2)
+            ys[s, two] = cs[s, c, 1 - yl, two] + cr[s, 1 - yl, two]
+            sent.append(remote(ys.at[s, two], yr.at[s, two], sy.at[s, part], ry.at[s, part], y_id))
         yo[s] = cs[s, c, yl] + cr[s, yl]
-        return [sent]
+        return sent
+
+    def z_copy(s, to, slot):
+        return pltpu.make_async_remote_copy(
+            src_ref=zs.at[s, to], dst_ref=zr.at[s, slot], send_sem=sz.at[s, to], recv_sem=rz.at[s, slot],
+            device_id=(o, (to * 2 + yl) * 2 + c), device_id_type=MESH,
+        )
 
     def z_start(s, copies):
-        copies[0].wait_recv()
         low = lax.broadcasted_iota(jnp.int32, (HB, TILE), 1) < TILE // 2
-        for zz in range(4):
-            first_half = yo[s, zz, 0:HB] + yr[s, zz, 0:HB]
-            second_half = yo[s, zz, HB:FB] + yr[s, zz, HB:FB]
-            zs[s, zz] = jnp.where(low, first_half, pltpu.roll(second_half, TILE // 2, 1))
-            zs[s, zz + 4] = jnp.where(low, pltpu.roll(first_half, TILE // 2, 1), second_half)
-        return [remote(zs.at[s, z_at[i]], zr.at[s, i], sz.at[s, i], rz.at[s, i], z_ids[i]) for i in range(7)]
-
-    def finish(s, copies):
-        for cp in copies:
-            cp.wait_recv()
+        for part in range(2):
+            copies[part].wait_recv()
+            for zz in (2 * part, 2 * part + 1):
+                first_half = yo[s, zz, 0:HB] + yr[s, zz, 0:HB]
+                second_half = yo[s, zz, HB:FB] + yr[s, zz, HB:FB]
+                zs[s, zz] = jnp.where(low, first_half, pltpu.roll(second_half, TILE // 2, 1))
+                zs[s, zz + 4] = jnp.where(low, pltpu.roll(first_half, TILE // 2, 1), second_half)
+            for to in (2 * part, 2 * part + 4, 2 * part + 1, 2 * part + 5):
+
+                @pl.when(to != z)
+                def _(to=to):
+                    z_copy(s, to, z).start()
+
+    def finish(s):
+        for other in z_at:
+            z_copy(s, other, other).wait_recv()
         total = zs[s, z]
-        for i in range(7):
-            total = total + zr[s, i]
+        for other in z_at:
+            total = total + zr[s, other]
         fs[s, 0:HB] = total
         flat = fs[s].T
         out[s, :, 0:HB] = flat[0:2 * R, 0:HB]
         out[s, :, HB:FB] = flat[2 * R:, 0:HB]
 
-    traces(0)
-    products(0, range(5))
+    own_row, other_row = row(yh), row(1 - yh)
+    traces(0, own_row, second[0][3:6])
+    products(0, own_row, range(5))
+    traces(0, other_row, second[0][0:3] + second[0][6:7])
+    products(0, other_row, range(5), more=True)
     core = [turn(0)]
-    traces(1)
-    products(1, range(3))
+    traces(1, whole, second[1])
+    products(1, whole, range(3))
     y = [y_start(0, core[0])]
-    products(1, range(3, 5))
+    products(1, whole, range(3, 5))
     core.append(turn(1))
-    traces(2)
-    products(2, range(3))
+    traces(2, whole, second[2])
+    products(2, whole, range(3))
     y.append(y_start(1, core[1]))
-    products(2, range(3, 5))
+    products(2, whole, range(3, 5))
     core.append(turn(2))
-    traces(3)
-    products(3, range(3))
+    traces(3, whole, second[3])
+    products(3, whole, range(3))
     y.append(y_start(2, core[2]))
-    zc = [z_start(0, y[0])]
-    products(3, range(3, 5))
+    z_start(0, y[0])
+    products(3, whole, range(3, 5))
     core.append(turn(3))
-    zc.append(z_start(1, y[1]))
+    z_start(1, y[1])
     y.append(y_start(3, core[3]))
-    zc.append(z_start(2, y[2]))
-    zc.append(z_start(3, y[3]))
+    z_start(2, y[2])
+    z_start(3, y[3])
     for s in range(S):
-        finish(s, zc[s])
-
-    for cp in first + rows + [cp for copies in second + core + y + zc for cp in copies]:
+        finish(s)
+
+    for cp in first + [cp for copies in second + core + y for cp in copies]:
         cp.wait_send()
+    for s in range(S):
+        for other in z_at:
+            z_copy(s, other, other).wait_send()
 
 
 def on_device(panels, shot_data, taper_table, destination, taper_level, shot_order):
@@ -303,11 +310,11 @@
             vmem((S, 4, FB, TILE), F32),
             vmem((S, 4, FB, TILE), F32),
             vmem((S, 8, HB, TILE), F32),
-            vmem((S, 7, HB, TILE), F32),
+            vmem((S, 8, HB, TILE), F32),
             vmem((S, TILE, TILE), F32),
             dma((4,)), dma, dma((R,)), dma,
-            dma((7,)), dma((7,)), dma((S, 7)), dma((S, 7)), dma((S, 3)), dma((S, 3)),
-            dma((S, 2)), dma((S, 2)), dma((S,)), dma((S,)), dma((S, 7)), dma((S, 7)),
+            dma((7,)), dma((7,)), dma((S, 7)), dma((S, 7)),
+            dma((S, 2)), dma((S, 2)), dma((S, 2)), dma((S, 2)), dma((S, 8)), dma((S, 8)),
         ],
         compiler_params=pltpu.CompilerParams(
             collective_id=0, has_side_effects=True, vmem_limit_bytes=48 * 2**20

time: 43.6 us -> 42.6 us (0.977)
  Pallas kernels: 42.9 us -> 41.9 us
    pallas_call x1, Pallas kernels: 42.9 us -> 41.9 us  [on_device(): pl.pallas_call(kernel, out_shape=jax.ShapeDtypeStruct((S, 2 * R, FB), F32...]
where the time goes in v3:
time: 42.6 us
  Pallas kernels  41.9 us (98%)
  local copies, waits for them, and re-layouts  0.66 us (2%)
    pallas_call x1, Pallas kernels, on_device(): pl.pallas_call(kernel, out_shape=jax.ShapeDtypeStruct((S, 2 * R, FB), F32...  41.9 us

profile of v3, /device:TPU:1, one launch (start us, length us, event | category | flops | bytes accessed | tf_op | source)
XLA Modules:
  0.0 42.6 jit_solution(14578076946763259195)
XLA Ops:
  0.0 41.9 %multiples.1 = f32[4,64,36]{2,1,0:T(8,128)S(1)} custom-call(bf16[40,32,2,1152]{3,2,1,0:T(2,128)(2,1)} %panels.1, bf16[2,40,2,1152]{3,2,1,0:T(2,128)(2,1)} %shots.1, f32[8,32]{1,0:T(8,128)} %table_hbm.1, s32[1,40]{1,0:T(1,128)} %dest_hbm.1, s32[1,40]{1,0:T(1,128)} %level_hbm.1, s32[4]{0:T(128)} %order_hbm.1), custom_call_target="tpu_custom_call" | custom-call | tf_op jit(solution)/shard_map/multiples/pallas_call | solution.py:284
  41.9 0.7 %copy.8 = f32[4,32,2,36]{3,2,1,0:T(2,128)} copy(f32[4,32,2,36]{3,2,1,0:T(2,128)S(1)} %bitcast.1) | data formatting | bytes 73728

commit v4 on v3

--- a/solution.py
+++ b/solution.py
@@ -24,7 +24,7 @@
 HB = FB // 2
 UNROLL = 20
 
-OUT_OFF = ((1, 1), (3, 1), (2, 1), (1, 0), (3, 0), (2, 0), (0, 1))
+OUT_OFF = ((2, 1), (1, 1), (3, 1), (2, 0), (1, 0), (3, 0), (0, 1))
 Z_OFF = (4, 3, 5, 2, 6, 1, 7)
 
 
@@ -248,20 +248,20 @@
     products(0, other_row, range(5), more=True)
     core = [turn(0)]
     traces(1, whole, second[1])
-    products(1, whole, range(3))
+    products(1, whole, range(4))
     y = [y_start(0, core[0])]
-    products(1, whole, range(3, 5))
+    products(1, whole, range(4, 5))
     core.append(turn(1))
     traces(2, whole, second[2])
-    products(2, whole, range(3))
+    products(2, whole, range(4))
     y.append(y_start(1, core[1]))
-    products(2, whole, range(3, 5))
+    products(2, whole, range(4, 5))
     core.append(turn(2))
     traces(3, whole, second[3])
-    products(3, whole, range(3))
+    products(3, whole, range(4))
     y.append(y_start(2, core[2]))
     z_start(0, y[0])
-    products(3, whole, range(3, 5))
+    products(3, whole, range(4, 5))
     core.append(turn(3))
     z_start(1, y[1])
     y.append(y_start(3, core[3]))

time: 42.6 us -> 42.2 us (level)
  no operation moved by 1% of the time
where the time goes in v4:
time: 42.2 us
  Pallas kernels  41.5 us (98%)
  local copies, waits for them, and re-layouts  0.66 us (2%)
    pallas_call x1, Pallas kernels, on_device(): pl.pallas_call(kernel, out_shape=jax.ShapeDtypeStruct((S, 2 * R, FB), F32...  41.5 us

profile of v4, /device:TPU:1, one launch (start us, length us, event | category | flops | bytes accessed | tf_op | source)
XLA Modules:
  0.0 42.2 jit_solution(12828697752750311806)
XLA Ops:
  0.0 41.5 %multiples.1 = f32[4,64,36]{2,1,0:T(8,128)S(1)} custom-call(bf16[40,32,2,1152]{3,2,1,0:T(2,128)(2,1)} %panels.1, bf16[2,40,2,1152]{3,2,1,0:T(2,128)(2,1)} %shots.1, f32[8,32]{1,0:T(8,128)} %table_hbm.1, s32[1,40]{1,0:T(1,128)} %dest_hbm.1, s32[1,40]{1,0:T(1,128)} %level_hbm.1, s32[4]{0:T(128)} %order_hbm.1), custom_call_target="tpu_custom_call" | custom-call | tf_op jit(solution)/shard_map/multiples/pallas_call | solution.py:284
  41.5 0.7 %copy.8 = f32[4,32,2,36]{3,2,1,0:T(2,128)} copy(f32[4,32,2,36]{3,2,1,0:T(2,128)S(1)} %bitcast.1) | data formatting | bytes 73728
